TPU v7x, 512 devices: a whole 4x8x8 slice. The times are simulated.
512 devices in a mesh: dp: 128 (over y, z, core), proto: 4 (over x).
Axes of the slice: x: 4, y: 8, z: 8, core: 2. Of those that a mesh axis runs over, the one named last changes fastest.
Arguments:
- embeddings: bfloat16 [2, 16384, 256], P(None, 'dp'), may hold values from -8 to 8
- prototypes: bfloat16 [256, 16384], P(None, 'proto'), may hold values from -0.375 to 0.375
Outputs:
- grad_embeddings: float32 [2, 16384, 256], P(None, 'dp')
- grad_prototypes: float32 [256, 16384], P('dp', 'proto')
All inputs are finite; a program needn't handle non-finite values.
Results may differ from a plain program's by a relative error of at most 0.0041.
The roundings to bfloat16 on the way count: a program that leaves them out, or rounds other values in their place, can miss the bound.
Values sent between devices are 32-bit elements; how exact they have to be, the bound alone decides.
A program may use at most 64 MiB of HBM per device.

v0:
```python
import jax
import jax.numpy as jnp
from jax import lax
from jax.sharding import PartitionSpec as P

ITERS = 2


sharpness_for_codebook = 0.05
guess_heat_inverse = 0.1


def unit_embed(values):
    return (
        values
        * lax.rsqrt(jnp.mean(values * values, axis=-1, keepdims=True) + 1e-06)
        * values.shape[-1] ** (-0.5)
    )


def unit_protos(prototypes):
    wide = prototypes.astype(jnp.float32)
    scaled = (
        wide
        * lax.rsqrt(jnp.mean(wide * wide, axis=0, keepdims=True) + 1e-06)
        * wide.shape[0] ** (-0.5)
    )
    return scaled.astype(jnp.bfloat16)


def shards(embeddings, prototypes):
    embed_wide = embeddings.astype(jnp.float32)
    unit_wide, pull_back = jax.vjp(unit_embed, embed_wide)
    unit_half = unit_wide.astype(jnp.bfloat16)
    proto_unit = unit_protos(prototypes)
    input_resemblances = [
        jnp.dot(unit_half[ongoing_augmented_input], proto_unit, preferred_element_type=jnp.float32)
        for ongoing_augmented_input in range(2)
    ]
    local_total = jnp.stack(
        [
            jnp.sum(jnp.exp(resemblance_patch / guess_heat_inverse), axis=-1)
            for resemblance_patch in input_resemblances
        ]
    )

    def column_pass(row_scaling):
        local_mass = jnp.stack(
            [
                jnp.sum(
                    jnp.exp(input_resemblances[ongoing_augmented_input] / sharpness_for_codebook)
                    * row_scaling[ongoing_augmented_input][:, None],
                    axis=0,
                )
                for ongoing_augmented_input in range(2)
            ]
        )
        return 1.0 / lax.psum(local_mass, "dp")

    def row_sums(column_scaling):
        return jnp.stack(
            [
                jnp.sum(
                    jnp.exp(input_resemblances[ongoing_augmented_input] / sharpness_for_codebook)
                    * column_scaling[ongoing_augmented_input][None, :],
                    axis=-1,
                )
                for ongoing_augmented_input in range(2)
            ]
        )

    row_scaling = jnp.ones(local_total.shape, jnp.float32)
    for sweep in range(ITERS):
        column_scaling = column_pass(row_scaling)
        row_scaling = 1.0 / lax.psum(row_sums(column_scaling), "proto")
    softmax_divisor = lax.psum(local_total, "proto")
    view_gradient_list = []
    for ongoing_augmented_input in range(2):
        sibling_crop = 1 - ongoing_augmented_input
        guessed_chances = (
            jnp.exp(input_resemblances[ongoing_augmented_input] / guess_heat_inverse)
            / softmax_divisor[ongoing_augmented_input][:, None]
        )
        wanted_group_soft_marks = (
            row_scaling[sibling_crop][:, None]
            * jnp.exp(input_resemblances[sibling_crop] / sharpness_for_codebook)
            * column_scaling[sibling_crop][None, :]
        )
        view_gradient_list.append(
            ((guessed_chances - wanted_group_soft_marks) / guess_heat_inverse).astype(jnp.bfloat16)
        )
    grad_partial = jnp.stack(
        [
            jnp.einsum(
                "rk,dk->rd",
                view_gradient_list[ongoing_augmented_input],
                proto_unit,
                preferred_element_type=jnp.float32,
            )
            for ongoing_augmented_input in range(2)
        ]
    )
    first = jnp.einsum(
        "rd,rk->dk", unit_half[0], view_gradient_list[0], preferred_element_type=jnp.float32
    )
    second = jnp.einsum(
        "rd,rk->dk", unit_half[1], view_gradient_list[1], preferred_element_type=jnp.float32
    )
    grad_prototypes = lax.psum_scatter(first + second, "dp", scatter_dimension=0, tiled=True)
    grad_unit = lax.psum(grad_partial, "proto")
    grad_embeddings = pull_back(grad_unit)[0]
    return (grad_embeddings, grad_prototypes)


def solution(mesh):
    placed = (P(None, "dp", None), P(None, "proto"))
    return jax.shard_map(
        shards,
        mesh=mesh,
        in_specs=placed,
        out_specs=(P(None, "dp", None), P("dp", "proto")),
        check_vma=False,
    )
```

profile of v0, /device:TPU:1, one launch (start us, length us, event | category | flops | bytes accessed | tf_op | source)
XLA Modules:
  0.0 1300.1 jit_solution(15930319779124918152)
XLA Ops:
  7.2 0.0 copy-start.3
  7.2 0.0 copy-start.4
  7.2 0.0 all-reduce.5.cloned.1.call-start
  7.2 2.2 fusion
  9.4 0.0 copy-done.3
  9.4 0.1 fusion.13
  9.6 0.1 fusion.15
  9.7 0.0 copy-done.4
  9.7 0.0 copy-start.5
  9.7 2.3 fusion.5
  12.0 0.0 copy-done.5
  12.0 0.9 fusion.6
  13.0 498.1 %psum.43 = f32[2,4096]{1,0:T(2,128)S(1)} all-reduce(f32[2,4096]{1,0:T(2,128)S(1)} %pad_maximum_fusion.1), channel_id=1, replica_groups=mesh['dp'=128,'proto'=4] {'dp'}, use_global_device_ids=true, to_apply=%region_7.0 | all-reduce | flops 8192 | bytes 65536 | tf_op jit(solution)/shard_map/psum | solution.py:58
  511.1 0.0 copy-start
  511.1 0.7 fusion.4
  511.8 0.8 copy-done
  512.6 0.7 fusion.3
  513.4 8.5 psum.44
  521.9 2.4 multiply_reduce_fusion.2
  524.3 492.9 %psum.45 = f32[2,4096]{1,0:T(2,128)S(1)} all-reduce(f32[2,4096]{1,0:T(2,128)S(1)} %pad_maximum_fusion.2), channel_id=1, replica_groups=mesh['dp'=128,'proto'=4] {'dp'}, use_global_device_ids=true, to_apply=%region_13.0 | all-reduce | flops 8192 | bytes 65536 | tf_op jit(solution)/shard_map/psum | solution.py:58
  1017.2 0.0 copy-start.1
  1017.3 0.4 multiply_reduce_fusion
  1017.7 1.1 copy-done.1
  1018.8 0.4 multiply_reduce_fusion.1
  1019.3 6.0 all-reduce.1
  1025.3 0.0 copy-start.6
  1025.3 3.1 multiply_convert_fusion.1
  1028.4 0.0 copy-start.2
  1028.5 0.0 copy-done.6
  1028.5 0.9 convolution_bitcast_fusion
  1029.3 0.1 copy-done.2
  1029.4 0.8 convolution_bitcast_fusion.1
  1030.3 0.7 pad_maximum_fusion
  1031.0 0.0 all-reduce.5.cloned.1.call-update
  1031.0 0.0 all-reduce.7.cloned.1.call-start
  1031.0 1.9 fusion.17
  1033.0 2.7 convolution_add_fusion
  1035.7 0.0 all-reduce.7.cloned.1.call-update
  1035.7 1.3 dynamic-slice
  1037.7 42.7 %all-reduce.5.cloned.1.call-done = f32[2,128,256]{2,1,0:T(8,128)} async-done(((f32[2,128,256]{2,1,0:T(8,128)}), f32[2,128,256]{2,1,0:T(8,128)}) %all-reduce.5.cloned.1.call-update) | async-done | bytes 262160 | tf_op jit(solution)/shard_map/psum | solution.py:110
  1080.4 1.1 fusion.16
  1081.5 1.8 add_add_fusion
  1083.2 208.5 %all-reduce.7.cloned.1.call-done = f32[256,4096]{1,0:T(8,128)} async-done(((f32[256,4096]{1,0:T(8,128)}), f32[256,4096]{1,0:T(8,128)}) %all-reduce.7.cloned.1.call-update) | async-done | bytes 4194320
  1291.8 1.5 constant_dynamic-slice_fusion
  (17 shorter events, 0.3 us)
Async XLA Ops:
  7.2 2.3 copy-start.3
  7.2 2.5 copy-start.4
  7.2 1073.2 %all-reduce.5.cloned.1.call-start = ((), (), s32[]{:S(2)}) async-start(), calls=%async_computation | async-start | bytes 524288 | tf_op jit(solution)/shard_map/psum | solution.py:110
  9.7 2.3 copy-start.5
  511.1 1.6 copy-start
  1017.2 1.6 copy-start.1
  1025.3 3.1 copy-start.6
  1028.4 1.0 copy-start.2
  1031.0 260.8 %all-reduce.7.cloned.1.call-start = ((), (), s32[]{:S(2)}) async-start(), calls=%async_computation.1 | async-start | bytes 8388608
Sparse Core Ops, SparseCore 0:
  1031.1 49.2 all-reduce.4
  1084.0 207.7 all-reduce.6
where the time goes:
time: 1300 us
  blocking collectives  1010 us (78%)
  waiting for transfers between devices  251 us (19%)
  between operations  14.9 us (1%)
  other arithmetic  14 us (1%)
    psum x2, blocking collectives, column_pass(): return 1.0 / lax.psum(local_mass, 'dp')  991 us
    unnamed x3, waiting for transfers between devices  209 us
    psum x1, waiting for transfers between devices, shards(): grad_unit = lax.psum(grad_partial, 'proto')  42.7 us
  transfers between devices with their start and end apart: 2, of which 2 were waited for; matrix products, arithmetic and copies ran while one was open for 1% of the time, Pallas kernels for 0%

commit v1 on v0

v1 whole, which is shorter than its diff:
```python
import jax
import jax.numpy as jnp
from jax import lax
from jax.experimental import pallas as pl
from jax.experimental.pallas import tpu as pltpu
from jax.sharding import PartitionSpec as P

MESH = pl.DeviceIdType.MESH
F32 = jnp.float32
BF16 = jnp.bfloat16

RING = 8
XS = 4
D = 256
COLS = 2048
HALF = 1024
CH = 512
ORDER = (4, 3, 5, 2, 6, 1, 7)


def place():
    dp = lax.axis_index("dp")
    x = lax.axis_index("proto")
    return lax.div(dp, 16), lax.rem(lax.div(dp, 2), RING), lax.rem(dp, 2), x


def device(y, z, c, x):
    return (y * 16 + z * 2 + c, x)


def kernel(
    emb_ref,
    proto_ref,
    ge_ref,
    gp_ref,
    praw,
    pn,
    usend,
    urecv,
    uall,
    ut,
    e_ref,
    cpart,
    csend,
    crecv,
    cvec,
    racc,
    rsend,
    rrecv,
    rb,
    zb,
    g_ref,
    gpart,
    rs_recv,
    p2send,
    p2recv,
    fin,
    fin_recv,
    gu_send,
    gu_recv,
    gx,
    gx_recv,
    gef,
    psem,
    ssem,
    rsem,
):
    y, z, c, x = place()
    used = [0]
    ends = []

    def sem():
        used[0] += 1
        return used[0] - 1

    def along(axis, s):
        if axis == "y":
            return device(lax.rem(y + s, RING), z, c, x)
        return device(y, lax.rem(z + s, RING), c, x)

    sibling = device(y, z, 1 - c, x)

    def remote(src, dst, k, target):
        return pltpu.make_async_remote_copy(
            src_ref=src,
            dst_ref=dst,
            send_sem=ssem.at[k],
            recv_sem=rsem.at[k],
            device_id=target,
            device_id_type=MESH,
        )

    def send(src, dst, target):
        k = sem()
        copy = remote(src, dst, k, target)
        copy.start()
        ends.append(copy.wait_send)
        return copy.wait_recv

    def fan(parts, whole):
        k = sem()
        for src, dst, target in parts:
            remote(src, dst, k, target).start()
        ends.append(lambda: pltpu.make_async_copy(whole, whole, ssem.at[k]).wait())
        return lambda: pltpu.make_async_copy(whole, whole, rsem.at[k]).wait()

    load = pltpu.make_async_copy(
        proto_ref.at[:, pl.ds(pl.multiple_of(c * COLS, COLS), COLS)], praw, psem
    )
    load.start()

    row_peers = [(s // 2, s % 2) for s in range(1, 2 * XS)]

    def row_peer(dx, dc):
        return device(y, z, lax.rem(c + dc, 2), lax.rem(x + dx, XS))

    barrier = pltpu.get_barrier_semaphore()
    peers = [along("y", s) for s in ORDER] + [along("z", s) for s in ORDER]
    peers += [row_peer(*p) for p in row_peers]
    for target in peers:
        pl.semaphore_signal(barrier, inc=1, device_id=target, device_id_type=MESH)

    def unit_rows(i, carry):
        wide = emb_ref[i].astype(F32)
        inv = lax.rsqrt(jnp.mean(wide * wide, axis=-1, keepdims=True) + 1e-06)
        half = (wide * inv * 0.0625).astype(BF16)
        rows = pl.ds(pl.multiple_of(i * 64, 64), 64)
        usend[rows, :] = half.astype(F32)
        uall[c, rows, :] = half
        return carry

    lax.fori_loop(0, 4, unit_rows, 0)
    load.wait()

    def unit_protos(i, carry):
        cols = pl.ds(pl.multiple_of(i * 256, 256), 256)
        wide = praw[:, cols].astype(F32)
        inv = lax.rsqrt(jnp.mean(wide * wide, axis=0, keepdims=True) + 1e-06)
        pn[:, cols] = (wide * inv * 0.0625).astype(BF16)
        return carry

    lax.fori_loop(0, COLS // 256, unit_protos, 0)

    def scores(slot, first):
        for v in range(2):
            def step(i, carry):
                cols = pl.ds(pl.multiple_of(i * 256, 256), 256)
                s = jnp.dot(
                    uall[slot, v * 128 : (v + 1) * 128, :], pn[:, cols], preferred_element_type=F32
                )
                e = jnp.exp(s * 10.0)
                e_ref[slot, v * 128 : (v + 1) * 128, cols] = e
                k = jnp.sum((e * e).reshape(16, 8, 256), axis=0)
                if first:
                    cpart[v, :, cols] = k
                else:
                    cpart[v, :, cols] += k
                return carry

            lax.fori_loop(0, COLS // 256, step, 0)

    scores(c, True)
    pl.semaphore_wait(barrier, len(peers))
    got_u = send(usend, urecv, sibling)
    got_u()
    uall[1 - c] = urecv[...].astype(BF16)
    scores(1 - c, False)

    def put_columns(it):
        for h in range(2):
            for v in range(2):
                csend[it, 0, h, v : v + 1, :] = jnp.sum(
                    cpart[v, :, h * HALF : (h + 1) * HALF], axis=0, keepdims=True
                )

    def columns(it):
        waits = []

        def go(ph, h):
            axis = "y" if (ph + h) % 2 == 0 else "z"
            return fan(
                [
                    (csend.at[it, ph, h], crecv.at[it, ph, h, s - 1], along(axis, s))
                    for s in ORDER
                ],
                crecv.at[it, ph, h],
            )

        for h in range(2):
            waits.append(go(0, h))
        again = []
        for h in range(2):
            waits[h]()
            total = csend[it, 0, h]
            for s in range(RING - 1):
                total = total + crecv[it, 0, h, s]
            csend[it, 1, h] = total
            again.append(go(1, h))
        for h in range(2):
            again[h]()
            total = csend[it, 1, h]
            for s in range(RING - 1):
                total = total + crecv[it, 1, h, s]
            cvec[:, h * HALF : (h + 1) * HALF] = 1.0 / total

    def row_pass(it):
        for slot in range(2):
            for v in range(2):
                def step(i, carry):
                    rows = pl.ds(pl.multiple_of(v * 128 + i * 32, 32), 32)
                    acc = jnp.zeros((32, 128), F32)
                    tot = jnp.zeros((32, 128), F32)
                    for t in range(COLS // 128):
                        e = e_ref[slot, rows, t * 128 : (t + 1) * 128]
                        acc = acc + e * e * cvec[v : v + 1, t * 128 : (t + 1) * 128]
                        if it == 0:
                            tot = tot + e
                    racc[0, slot * 2 + v, pl.ds(pl.multiple_of(i * 32, 32), 32), :] = acc
                    if it == 0:
                        racc[1, slot * 2 + v, pl.ds(pl.multiple_of(i * 32, 32), 32), :] = tot
                    return carry

                lax.fori_loop(0, 4, step, 0)
        for w in range(2):
            for q in range(4):
                if it == 0 or w == 0:
                    row = jnp.sum(racc[w, q].T, axis=0, keepdims=True)
                else:
                    row = jnp.zeros((1, 128), F32)
                rsend[it, w * 4 + q : w * 4 + q + 1, :] = row

    def row_exchange(it):
        got = fan(
            [(rsend.at[it], rrecv.at[it, i], row_peer(*p)) for i, p in enumerate(row_peers)],
            rrecv.at[it],
        )
        got()
        total = rsend[it]
        for i in range(len(row_peers)):
            total = total + rrecv[it, i]
        scale = 1.0 / total
        for q in range(4):
            rb[q] = jnp.broadcast_to(scale[q : q + 1, :], (128, 128)).T
            if it == 0:
                zb[q] = jnp.broadcast_to(scale[4 + q : 5 + q, :], (128, 128)).T

    def column_pass():
        def step(i, carry):
            base = i * 512
            for v in range(2):
                acc = [jnp.zeros((8, 128), F32) for _ in range(4)]

                def rows8(j, acc):
                    acc = list(acc)
                    for slot in range(2):
                        for w in range(2):
                            r0 = pl.multiple_of(j * 16 + w * 8, 8)
                            r = rb[slot * 2 + v, pl.ds(r0, 8), :]
                            for t in range(4):
                                cols = pl.ds(pl.multiple_of(base + t * 128, 128), 128)
                                e = e_ref[slot, pl.ds(pl.multiple_of(v * 128 + r0, 8), 8), cols]
                                acc[t] = acc[t] + e * e * r
                    return tuple(acc)

                acc = lax.fori_loop(0, 8, rows8, tuple(acc))
                for t in range(4):
                    cols = pl.ds(pl.multiple_of(base + t * 128, 128), 128)
                    cpart[v, :, cols] = acc[t]
            return carry

        lax.fori_loop(0, COLS // 512, step, 0)

    put_columns(0)
    columns(0)
    row_pass(0)
    row_exchange(0)
    column_pass()
    put_columns(1)
    columns(1)
    row_pass(1)

    to = lax.broadcasted_iota(jnp.int32, (D, D), 0)
    at = lax.broadcasted_iota(jnp.int32, (D, D), 1)
    natural = (to == at).astype(BF16)
    swapped = ((to // 32) * 4 + ((to // 4) % 8) * 32 + to % 4 == at).astype(BF16)
    for h, order in ((0, natural), (1, swapped)):
        for slot in range(2):
            ut[h, :, slot * 256 : (slot + 1) * 256] = lax.dot_general(
                order, uall[slot], (((1,), (1,)), ((), ())), preferred_element_type=F32
            ).astype(BF16)

    row_exchange(1)

    chunks = [
        ("y", "z", 0, 0, 4, 3),
        ("z", "y", 1, HALF, 4, 3),
        ("y", "z", 0, CH, 3, 4),
        ("z", "y", 1, HALF + CH, 3, 4),
    ]
    own = {"y": y, "z": z}

    def slab(ch, axis, s):
        which = lax.rem(own[axis] + (s + RING), RING)
        return gpart.at[ch, pl.ds(pl.multiple_of(which * 32, 32), 32), :]

    def slot_of(ch, sign, i):
        return i if sign > 0 else chunks[ch][4] + i

    flight = {}

    def hop(ch, sign, i, src):
        axis = chunks[ch][0]
        flight[ch, sign, i] = send(
            src, rs_recv.at[ch, slot_of(ch, sign, i)], along(axis, sign % RING)
        )

    for ch, (axis, _, h, col0, plus, minus) in enumerate(chunks):
        for slot in range(2):
            def step(i, carry):
                r0 = pl.multiple_of(i * 16, 16)
                rows0 = pl.ds(r0, 16)
                rows1 = pl.ds(pl.multiple_of(128 + r0, 16), 16)
                ra = rb[slot * 2, rows0, :] * 10.0
                rc = rb[slot * 2 + 1, rows0, :] * 10.0
                za = zb[slot * 2, rows0, :] * 10.0
                zc = zb[slot * 2 + 1, rows0, :] * 10.0
                for t in range(CH // 128):
                    cols = slice(col0 + t * 128, col0 + (t + 1) * 128)
                    e0 = e_ref[slot, rows0, cols]
                    e1 = e_ref[slot, rows1, cols]
                    k0 = e0 * e0 * cvec[0:1, cols]
                    k1 = e1 * e1 * cvec[1:2, cols]
                    g_ref[slot, rows0, cols] = (e0 * za - k1 * rc).astype(BF16)
                    g_ref[slot, rows1, cols] = (e1 * zc - k0 * ra).astype(BF16)
                return carry

            lax.fori_loop(0, 8, step, 0)
        gpart[ch] = jnp.dot(
            ut[h, :, 0:256], g_ref[0, :, col0 : col0 + CH], preferred_element_type=F32
        ) + jnp.dot(
            ut[h, :, 256:512], g_ref[1, :, col0 : col0 + CH], preferred_element_type=F32
        )
        hop(ch, 1, 0, slab(ch, axis, plus))
        hop(ch, -1, 0, slab(ch, axis, -minus))

    def back(slot):
        return lax.dot_general(
            g_ref[slot], pn[...], (((1,), (1,)), ((), ())), preferred_element_type=F32
        )

    def advance(i):
        for ch, (axis, _, _, _, plus, minus) in enumerate(chunks):
            for sign, length in ((1, plus), (-1, minus)):
                if i >= length:
                    continue
                flight[ch, sign, i]()
                left = length - 1 - i
                if left:
                    here = rs_recv.at[ch, slot_of(ch, sign, i)]
                    here[...] = here[...] + slab(ch, axis, sign * left)[...]
                    hop(ch, sign, i + 1, here)

    gu_send[...] = back(1 - c)
    got_gu = send(gu_send, gu_recv, sibling)
    gx[...] = back(c).reshape(4, 64, 256)

    advance(0)

    got_gu()
    gx[...] = gx[...] + gu_recv[...].reshape(4, 64, 256)

    def along_x(s):
        return device(y, z, c, lax.rem(x + s, XS))

    got_gx = fan(
        [(gx.at[lax.rem(x + s, XS)], gx_recv.at[s - 1], along_x(s)) for s in (2, 1, 3)], gx_recv
    )

    advance(1)
    advance(2)

    got_gx()
    g = gx[x] + gx_recv[0] + gx_recv[1] + gx_recv[2]
    wide = emb_ref[x].astype(F32)
    inv = lax.rsqrt(jnp.mean(wide * wide, axis=-1, keepdims=True) + 1e-06)
    mean = jnp.mean(wide * g, axis=-1, keepdims=True)
    gef[x] = (g * inv - wide * (inv * inv * inv * mean)) * 0.0625
    got_ge = [send(gef.at[x], gef.at[x], along_x(s)) for s in (2, 1, 3)]

    got_p2 = {}
    for ch, (axis, axis2, _, _, plus, minus) in enumerate(chunks):
        for sign, length in ((1, plus), (-1, minus)):
            if length == 4:
                flight[ch, sign, 3]()
        total = (
            slab(ch, axis, 0)[...]
            + rs_recv[ch, slot_of(ch, 1, plus - 1)]
            + rs_recv[ch, slot_of(ch, -1, minus - 1)]
        )
        for q in range(RING):
            p2send[ch, q] = total[q * 4 : q * 4 + 4, :]
        got_p2[ch] = fan(
            [
                (p2send.at[ch, lax.rem(own[axis2] + s, RING)], p2recv.at[ch, s - 1], along(axis2, s))
                for s in ORDER
            ],
            p2recv.at[ch],
        )

    for wait in got_ge:
        wait()
    ge_ref[...] = gef[...]

    for ch, (_, axis2, _, col0, _, _) in enumerate(chunks):
        got_p2[ch]()
        total = p2send[ch, own[axis2]]
        for s in range(RING - 1):
            total = total + p2recv[ch, s]
        for q in range(2):
            fin[q, :, col0 : col0 + CH] = total[q * 2 : q * 2 + 2, :]
    got_fin = send(fin.at[1 - c], fin_recv, sibling)
    gp_ref[:, pl.ds(pl.multiple_of(c * COLS, COLS), COLS)] = fin[c]
    got_fin()
    gp_ref[:, pl.ds(pl.multiple_of((1 - c) * COLS, COLS), COLS)] = fin_recv[...]

    for wait in ends:
        wait()
    assert used[0] <= SEMS


SEMS = 64


def shards(embeddings, prototypes):
    vmem = pl.BlockSpec(memory_space=pltpu.VMEM)
    ge, gp = pl.pallas_call(
        kernel,
        name="swap_step",
        out_shape=(
            jax.ShapeDtypeStruct((4, 64, D), F32),
            jax.ShapeDtypeStruct((2, 2 * COLS), F32),
        ),
        in_specs=[vmem, pl.BlockSpec(memory_space=pl.ANY)],
        out_specs=(vmem, vmem),
        scratch_shapes=[
            pltpu.VMEM((D, COLS), BF16),
            pltpu.VMEM((D, COLS), BF16),
            pltpu.VMEM((256, D), F32),
            pltpu.VMEM((256, D), F32),
            pltpu.VMEM((2, 256, D), BF16),
            pltpu.VMEM((2, D, 512), BF16),
            pltpu.VMEM((2, 256, COLS), F32),
            pltpu.VMEM((2, 8, COLS), F32),
            pltpu.VMEM((2, 2, 2, 2, HALF), F32),
            pltpu.VMEM((2, 2, 2, RING - 1, 2, HALF), F32),
            pltpu.VMEM((2, COLS), F32),
            pltpu.VMEM((2, 4, 128, 128), F32),
            pltpu.VMEM((2, 8, 128), F32),
            pltpu.VMEM((2, 2 * XS - 1, 8, 128), F32),
            pltpu.VMEM((4, 128, 128), F32),
            pltpu.VMEM((4, 128, 128), F32),
            pltpu.VMEM((2, 256, COLS), BF16),
            pltpu.VMEM((4, D, CH), F32),
            pltpu.VMEM((4, 7, 32, CH), F32),
            pltpu.VMEM((4, RING, 4, CH), F32),
            pltpu.VMEM((4, RING - 1, 4, CH), F32),
            pltpu.VMEM((2, 2, COLS), F32),
            pltpu.VMEM((2, COLS), F32),
            pltpu.VMEM((256, D), F32),
            pltpu.VMEM((256, D), F32),
            pltpu.VMEM((4, 64, D), F32),
            pltpu.VMEM((3, 64, D), F32),
            pltpu.VMEM((4, 64, D), F32),
            pltpu.SemaphoreType.DMA,
            pltpu.SemaphoreType.DMA((SEMS,)),
            pltpu.SemaphoreType.DMA((SEMS,)),
        ],
        compiler_params=pltpu.CompilerParams(
            collective_id=0, has_side_effects=True, vmem_limit_bytes=40 << 20
        ),
        cost_estimate=pl.CostEstimate(
            flops=2_000_000_000, bytes_accessed=4_000_000, transcendentals=1_100_000
        ),
    )(embeddings.reshape(4, 64, D), prototypes)
    return ge.reshape(2, 128, D), gp


def solution(mesh):
    return jax.shard_map(
        shards,
        mesh=mesh,
        in_specs=(P(None, "dp", None), P(None, "proto")),
        out_specs=(P(None, "dp", None), P("dp", "proto")),
        check_vma=False,
    )
```

time: 1300 us -> 80.1 us (0.06)
  blocking collectives: 1010 us -> 0 us
  waiting for transfers between devices: 251 us -> 0 us
  Pallas kernels: 0 us -> 75.4 us
  between operations: 14.9 us -> 0.65 us
  other arithmetic: 14 us -> 0 us
    psum x4 -> x0, blocking collectives: 1010 us -> none  [the longest x2 991 us: column_pass(): return 1.0 / lax.psum(local_mass, 'dp')]
    unnamed x3 -> x0, waiting for transfers between devices: 209 us -> none
    pallas_call x0 -> x1, Pallas kernels: none -> 75.4 us  [shards(): pl.pallas_call(kernel, name='swap_step', out_shape=(jax.ShapeDtypeStruct(...]
    psum x1 -> x0, waiting for transfers between devices: 42.7 us -> none  [shards(): grad_unit = lax.psum(grad_partial, 'proto')]
  transfers between devices with their start and end apart: 2 -> 0, of which waited for: 2 -> 0; matrix products, arithmetic and copies ran while one was open for 1% -> 0% of each run, Pallas kernels for 0% -> 0%
where the time goes in v1:
time: 80.1 us; the launch traced here: 79.9 us
  Pallas kernels  75.4 us (94%)
  local copies, waits for them, and re-layouts  3.81 us (5%)
    pallas_call x1, Pallas kernels, shards(): pl.pallas_call(kernel, name='swap_step', out_shape=(jax.ShapeDtypeStruct(...  75.4 us
    unnamed x6, local copies, waits for them, and re-layouts  3.81 us

profile of v1, /device:TPU:1, one launch (start us, length us, event | category | flops | bytes accessed | tf_op | source)
XLA Modules:
  0.0 79.9 jit_solution(10451231543127684352)
XLA Ops:
  0.6 0.0 copy-start
  0.6 1.6 %copy-done = bf16[256,4096]{1,0:T(8,128)(2,1)S(1)} copy-done((bf16[256,4096]{1,0:T(8,128)(2,1)S(1)}, bf16[256,4096]{1,0:T(8,128)(2,1)}, u32[]{:S(2)}) %copy-start) | copy-done | bytes 2097176
  2.2 0.0 copy-start.1
  2.2 0.9 %copy-done.1 = bf16[2,128,256]{2,1,0:T(8,128)(2,1)S(1)} copy-done((bf16[2,128,256]{2,1,0:T(8,128)(2,1)S(1)}, bf16[2,128,256]{2,1,0:T(8,128)(2,1)}, u32[]{:S(2)}) %copy-start.1) | copy-done | bytes 131096
  3.1 75.4 %swap_step.1 = (f32[4,64,256]{2,1,0:T(8,128)S(1)}, f32[2,4096]{1,0:T(2,128)S(1)}) custom-call(bf16[4,64,256]{2,1,0:T(8,128)(2,1)S(1)} %bitcast.3, bf16[256,4096]{1,0:T(8,128)(2,1)S(1)} %copy-done), custom_call_target="tpu_custom_call" | custom-call | flops 2000000000 | bytes 4000000 | tf_op jit(solution)/shard_map/swap_step/pallas_call | solution.py:436
  78.6 0.7 copy.6
  79.3 0.6 copy.7
Async XLA Ops:
  0.6 1.6 %copy-start = (bf16[256,4096]{1,0:T(8,128)(2,1)S(1)}, bf16[256,4096]{1,0:T(8,128)(2,1)}, u32[]{:S(2)}) copy-start(bf16[256,4096]{1,0:T(8,128)(2,1)} %proto_ref.1) | copy-start | bytes 6291460
  2.2 0.9 %copy-start.1 = (bf16[2,128,256]{2,1,0:T(8,128)(2,1)S(1)}, bf16[2,128,256]{2,1,0:T(8,128)(2,1)}, u32[]{:S(2)}) copy-start(bf16[2,128,256]{2,1,0:T(8,128)(2,1)} %param.2) | copy-start | bytes 393220

commit v2 on v1

v2 whole, which is shorter than its diff:
```python
import jax
import jax.numpy as jnp
from jax import lax
from jax.experimental import pallas as pl
from jax.experimental.pallas import tpu as pltpu
from jax.sharding import PartitionSpec as P

MESH = pl.DeviceIdType.MESH
F32 = jnp.float32
BF16 = jnp.bfloat16

RING = 8
XS = 4
D = 256
COLS = 2048
HALF = 1024
CH = 256
ORDER = (4, 3, 5, 2, 6, 1, 7)


def place():
    dp = lax.axis_index("dp")
    x = lax.axis_index("proto")
    return lax.div(dp, 16), lax.rem(lax.div(dp, 2), RING), lax.rem(dp, 2), x


def device(y, z, c, x):
    return (y * 16 + z * 2 + c, x)


def kernel(
    emb_hbm,
    proto_ref,
    ge_ref,
    gp_ref,
    emb_ref,
    praw,
    pn,
    usend,
    urecv,
    uall,
    ut,
    e_ref,
    m_ref,
    cpart,
    csend,
    crecv,
    cvec,
    racc,
    rsend,
    rrecv,
    rb,
    zb,
    g_ref,
    gpart,
    rs_recv,
    p2send,
    p2recv,
    fin,
    fin_recv,
    gu_send,
    gu_recv,
    gx,
    gx_recv,
    gef,
    psem,
    ssem,
    rsem,
):
    y, z, c, x = place()
    used = [0]
    ends = []

    def sem():
        used[0] += 1
        return used[0] - 1

    def along(axis, s):
        if axis == "y":
            return device(lax.rem(y + s, RING), z, c, x)
        return device(y, lax.rem(z + s, RING), c, x)

    sibling = device(y, z, 1 - c, x)

    def remote(src, dst, k, target):
        return pltpu.make_async_remote_copy(
            src_ref=src,
            dst_ref=dst,
            send_sem=ssem.at[k],
            recv_sem=rsem.at[k],
            device_id=target,
            device_id_type=MESH,
        )

    def send(src, dst, target):
        k = sem()
        copy = remote(src, dst, k, target)
        copy.start()
        ends.append(copy.wait_send)
        return copy.wait_recv

    def fan(parts, whole):
        k = sem()
        for src, dst, target in parts:
            remote(src, dst, k, target).start()
        ends.append(lambda: pltpu.make_async_copy(whole, whole, ssem.at[k]).wait())
        return lambda: pltpu.make_async_copy(whole, whole, rsem.at[k]).wait()

    load_emb = pltpu.make_async_copy(emb_hbm, emb_ref, psem.at[0])
    load_emb.start()
    load = pltpu.make_async_copy(
        proto_ref.at[:, pl.ds(pl.multiple_of(c * COLS, COLS), COLS)], praw, psem.at[1]
    )
    load.start()

    row_peers = [(s // 2, s % 2) for s in range(1, 2 * XS)]

    def row_peer(dx, dc):
        return device(y, z, lax.rem(c + dc, 2), lax.rem(x + dx, XS))

    barrier = pltpu.get_barrier_semaphore()
    peers = [along("y", s) for s in ORDER] + [along("z", s) for s in ORDER]
    peers += [row_peer(*p) for p in row_peers]
    for target in peers:
        pl.semaphore_signal(barrier, inc=1, device_id=target, device_id_type=MESH)

    def unit_rows(i, carry):
        wide = emb_ref[i].astype(F32)
        inv = lax.rsqrt(jnp.mean(wide * wide, axis=-1, keepdims=True) + 1e-06)
        half = (wide * inv * 0.0625).astype(BF16)
        rows = pl.ds(pl.multiple_of(i * 64, 64), 64)
        usend[rows, :] = half.astype(F32)
        uall[c, rows, :] = half
        return carry

    load_emb.wait()
    lax.fori_loop(0, 4, unit_rows, 0)
    load.wait()

    def unit_protos(i, carry):
        cols = pl.ds(pl.multiple_of(i * 256, 256), 256)
        wide = praw[:, cols].astype(F32)
        inv = lax.rsqrt(jnp.mean(wide * wide, axis=0, keepdims=True) + 1e-06)
        pn[:, cols] = (wide * inv * 0.0625).astype(BF16)
        return carry

    lax.fori_loop(0, COLS // 256, unit_protos, 0)

    def scores(slot, first, lo, hi):
        def step(i, carry):
            cols = pl.ds(pl.multiple_of(i * 512, 512), 512)
            s = jnp.dot(uall[slot], pn[:, cols], preferred_element_type=F32)
            e = jnp.exp(s * 10.0)
            for v in range(2):
                part = e[v * 128 : (v + 1) * 128, :]
                e_ref[slot * 2 + v, :, cols] = part
                k = jnp.sum((part * part).reshape(16, 8, 512), axis=0)
                if first:
                    cpart[v, :, cols] = k
                else:
                    cpart[v, :, cols] += k
            return carry

        lax.fori_loop(lo, hi, step, 0)

    scores(c, True, 0, 2)
    pl.semaphore_wait(barrier, len(peers))
    got_u = send(usend, urecv, sibling)
    scores(c, True, 2, 4)
    got_u()
    uall[1 - c] = urecv[...].astype(BF16)

    def columns_start(it, h):
        for v in range(2):
            for t in range(8):
                col = h * HALF + t * 128
                csend[it, 0, h, v, t : t + 1, :] = jnp.sum(
                    cpart[v, :, col : col + 128], axis=0, keepdims=True
                )
        return columns_go(it, 0, h)

    def columns_go(it, ph, h):
        axis = "y" if (ph + h) % 2 == 0 else "z"
        return fan(
            [(csend.at[it, ph, h], crecv.at[it, ph, h, s - 1], along(axis, s)) for s in ORDER],
            crecv.at[it, ph, h],
        )

    def columns_sum(it, ph, h):
        total = csend[it, ph, h]
        for s in range(RING - 1):
            total = total + crecv[it, ph, h, s]
        return total

    def columns_next(it, h):
        csend[it, 1, h] = columns_sum(it, 0, h)
        return columns_go(it, 1, h)

    def columns_end(it, h):
        cvec[:, h * 8 : h * 8 + 8, :] = 1.0 / columns_sum(it, 1, h)

    def row_pass(it, h):
        def step(i, carry):
            q = lax.div(i, 2)
            v = lax.rem(q, 2)
            rows = pl.ds(pl.multiple_of(lax.rem(i, 2) * 64, 64), 64)
            if h == 0:
                acc = jnp.zeros((64, 128), F32)
                tot = jnp.zeros((64, 128), F32)
            else:
                acc = racc[0, q, rows, :]
                tot = racc[1, q, rows, :] if it == 0 else None
            for t in range(h * 8, h * 8 + 8):
                e = e_ref[q, rows, t * 128 : (t + 1) * 128]
                acc = acc + e * e * cvec[v, t : t + 1, :]
                if it == 0:
                    tot = tot + e
            racc[0, q, rows, :] = acc
            if it == 0:
                racc[1, q, rows, :] = tot
            return carry

        lax.fori_loop(0, 8, step, 0)

    def row_start(it):
        for w in range(2):
            for q in range(4):
                if it == 0 or w == 0:
                    row = jnp.sum(racc[w, q].T, axis=0, keepdims=True)
                else:
                    row = jnp.zeros((1, 128), F32)
                rsend[it, w * 4 + q : w * 4 + q + 1, :] = row
        return fan(
            [(rsend.at[it], rrecv.at[it, i], row_peer(*p)) for i, p in enumerate(row_peers)],
            rrecv.at[it],
        )

    def row_end(it):
        total = rsend[it]
        for i in range(len(row_peers)):
            total = total + rrecv[it, i]
        scale = 1.0 / total
        if it == 1:
            scale = scale * 10.0
        for q in range(4):
            rb[q] = jnp.broadcast_to(scale[q : q + 1, :], (128, 128)).T
            if it == 0:
                zb[q] = jnp.broadcast_to(scale[4 + q : 5 + q, :] * 10.0, (128, 128)).T

    def column_pass(h):
        def step(i, carry):
            v = lax.rem(i, 2)
            base = h * HALF + lax.div(i, 2) * 512
            acc = [jnp.zeros((8, 128), F32) for _ in range(4)]

            def rows32(j, acc):
                acc = list(acc)
                for slot in range(2):
                    for w in range(4):
                        rows = pl.ds(pl.multiple_of(j * 32 + w * 8, 8), 8)
                        r = rb[slot * 2 + v, rows, :]
                        for t in range(4):
                            cols = pl.ds(pl.multiple_of(base + t * 128, 128), 128)
                            e = e_ref[slot * 2 + v, rows, cols]
                            acc[t] = acc[t] + e * e * r
                return tuple(acc)

            acc = lax.fori_loop(0, 4, rows32, tuple(acc))
            for t in range(4):
                cols = pl.ds(pl.multiple_of(base + t * 128, 128), 128)
                cpart[v, :, cols] = acc[t]
            return carry

        lax.fori_loop(0, 4, step, 0)

    scores(1 - c, False, 0, 2)
    first_a = columns_start(0, 0)
    scores(1 - c, False, 2, 4)
    first_b = columns_start(0, 1)
    for it in range(2):
        first_a()
        second_a = columns_next(it, 0)
        first_b()
        second_b = columns_next(it, 1)
        second_a()
        columns_end(it, 0)
        row_pass(it, 0)
        second_b()
        columns_end(it, 1)
        row_pass(it, 1)
        got_rows = row_start(it)
        if it == 0:
            got_rows()
            row_end(it)
            column_pass(0)
            first_a = columns_start(1, 0)
            column_pass(1)
            first_b = columns_start(1, 1)

    def scaled(i, carry):
        q = lax.div(i, 4)
        v = lax.rem(q, 2)
        rows = pl.ds(pl.multiple_of(lax.rem(i, 4) * 32, 32), 32)
        zr = zb[q, rows, :]
        for t in range(COLS // 128):
            cols = slice(t * 128, (t + 1) * 128)
            e = e_ref[q, rows, cols]
            m_ref[q, rows, cols] = e * e * cvec[v, t : t + 1, :]
            e_ref[q, rows, cols] = e * zr
        return carry

    lax.fori_loop(0, 16, scaled, 0)

    to = lax.broadcasted_iota(jnp.int32, (D, D), 0)
    at = lax.broadcasted_iota(jnp.int32, (D, D), 1)
    natural = (to == at).astype(BF16)
    swapped = ((to // 32) * 4 + ((to // 4) % 8) * 32 + to % 4 == at).astype(BF16)
    for h, order in ((0, natural), (1, swapped)):
        for slot in range(2):
            ut[h, :, slot * 256 : (slot + 1) * 256] = lax.dot_general(
                order, uall[slot], (((1,), (1,)), ((), ())), preferred_element_type=F32
            ).astype(BF16)

    got_rows()
    row_end(1)

    chunks = []
    for j in range(HALF // CH):
        sign = 1 if j % 2 == 0 else -1
        chunks.append(("y", "z", 0, j * CH, sign))
        chunks.append(("z", "y", 1, HALF + j * CH, sign))
    own = {"y": y, "z": z}

    def slab(ch, s):
        which = lax.rem(own[chunks[ch][0]] + (s + RING), RING)
        return gpart.at[ch, pl.ds(pl.multiple_of(which * 32, 32), 32), :]

    flight = {}

    def hop(ch, way, src, s):
        flight[ch, way] = send(src, rs_recv.at[ch, way], along(chunks[ch][0], s % RING))

    def step0(ch):
        sign = chunks[ch][4]
        hop(ch, 6, slab(ch, 4 * sign), 2 * sign)
        hop(ch, 0, slab(ch, 3 * sign), sign)
        hop(ch, 3, slab(ch, -3 * sign), -sign)

    def step1(ch):
        sign = chunks[ch][4]
        flight[ch, 3]()
        here = rs_recv.at[ch, 3]
        here[...] = here[...] + slab(ch, -2 * sign)[...]
        hop(ch, 4, here, -sign)
        flight[ch, 0]()
        flight[ch, 6]()
        here = rs_recv.at[ch, 0]
        here[...] = here[...] + rs_recv[ch, 6] + slab(ch, 2 * sign)[...]
        hop(ch, 1, here, sign)

    def step2(ch):
        for way, sign in ((1, chunks[ch][4]), (4, -chunks[ch][4])):
            flight[ch, way]()
            here = rs_recv.at[ch, way]
            here[...] = here[...] + slab(ch, sign)[...]
            hop(ch, way + 1, here, sign)

    got_p2 = {}

    def step3(ch):
        axis2 = chunks[ch][1]
        flight[ch, 2]()
        flight[ch, 5]()
        total = slab(ch, 0)[...] + rs_recv[ch, 2] + rs_recv[ch, 5]
        for q in range(RING):
            p2send[ch, q] = total[q * 4 : q * 4 + 4, :]
        got_p2[ch] = fan(
            [
                (p2send.at[ch, lax.rem(own[axis2] + s, RING)], p2recv.at[ch, s - 1], along(axis2, s))
                for s in ORDER
            ],
            p2recv.at[ch],
        )

    for ch, (_, _, h, col0, _) in enumerate(chunks):
        def terms(i, carry):
            slot = lax.div(i, 2)
            for v in range(2):
                q = slot * 2 + v
                o = slot * 2 + 1 - v
                for w in range(2):
                    row0 = lax.rem(i, 2) * 64 + w * 32
                    rows = pl.ds(pl.multiple_of(row0, 32), 32)
                    r = rb[o, rows, :]
                    to_rows = pl.ds(pl.multiple_of(q * 128 + row0, 32), 32)
                    for t in range(CH // 128):
                        cols = slice(col0 + t * 128, col0 + (t + 1) * 128)
                        g_ref[to_rows, cols] = (
                            e_ref[q, rows, cols] - m_ref[o, rows, cols] * r
                        ).astype(BF16)
            return carry

        lax.fori_loop(0, 4, terms, 0)
        gpart[ch] = jnp.dot(ut[h], g_ref[:, col0 : col0 + CH], preferred_element_type=F32)
        step0(ch)

    def back(slot):
        return lax.dot_general(
            g_ref[pl.ds(pl.multiple_of(slot * 256, 256), 256), :],
            pn[...],
            (((1,), (1,)), ((), ())),
            preferred_element_type=F32,
        )

    def along_x(s):
        return device(y, z, c, lax.rem(x + s, XS))

    gu_send[...] = back(1 - c)
    got_gu = send(gu_send, gu_recv, sibling)
    gx[...] = back(c).reshape(4, 64, 256)
    for ch in range(len(chunks) // 2):
        step1(ch)
    got_gu()
    gx[...] = gx[...] + gu_recv[...].reshape(4, 64, 256)
    got_gx = fan(
        [(gx.at[lax.rem(x + s, XS)], gx_recv.at[s - 1], along_x(s)) for s in (2, 1, 3)], gx_recv
    )
    for ch in range(len(chunks) // 2, len(chunks)):
        step1(ch)
    for ch in range(len(chunks)):
        step2(ch)
    for ch in range(len(chunks) // 2):
        step3(ch)

    got_gx()
    g = gx[x] + gx_recv[0] + gx_recv[1] + gx_recv[2]
    wide = emb_ref[x].astype(F32)
    inv = lax.rsqrt(jnp.mean(wide * wide, axis=-1, keepdims=True) + 1e-06)
    mean = jnp.mean(wide * g, axis=-1, keepdims=True)
    gef[x] = (g * inv - wide * (inv * inv * inv * mean)) * 0.0625
    got_ge = [send(gef.at[x], gef.at[x], along_x(s)) for s in (2, 1, 3)]

    for ch in range(len(chunks) // 2, len(chunks)):
        step3(ch)

    def second(ch):
        _, axis2, _, col0, _ = chunks[ch]
        got_p2[ch]()
        total = p2send[ch, own[axis2]]
        for s in range(RING - 1):
            total = total + p2recv[ch, s]
        for q in range(2):
            fin[q, :, col0 : col0 + CH] = total[q * 2 : q * 2 + 2, :]

    for ch in range(len(chunks)):
        second(ch)
    got_fin = send(fin.at[1 - c], fin_recv, sibling)
    gp_ref[:, pl.ds(pl.multiple_of(c * COLS, COLS), COLS)] = fin[c]
    for wait in got_ge:
        wait()
    ge_ref[...] = gef[...]
    got_fin()
    gp_ref[:, pl.ds(pl.multiple_of((1 - c) * COLS, COLS), COLS)] = fin_recv[...]

    for wait in ends:
        wait()
    assert used[0] <= SEMS


SEMS = 96


def shards(embeddings, prototypes):
    vmem = pl.BlockSpec(memory_space=pltpu.VMEM)
    ge, gp = pl.pallas_call(
        kernel,
        name="swap_step",
        out_shape=(
            jax.ShapeDtypeStruct((4, 64, D), F32),
            jax.ShapeDtypeStruct((2, 2 * COLS), F32),
        ),
        in_specs=[pl.BlockSpec(memory_space=pltpu.HBM)] * 2,
        out_specs=(vmem, vmem),
        scratch_shapes=[
            pltpu.VMEM((4, 64, D), BF16),
            pltpu.VMEM((D, COLS), BF16),
            pltpu.VMEM((D, COLS), BF16),
            pltpu.VMEM((256, D), F32),
            pltpu.VMEM((256, D), F32),
            pltpu.VMEM((2, 256, D), BF16),
            pltpu.VMEM((2, D, 512), BF16),
            pltpu.VMEM((4, 128, COLS), F32),
            pltpu.VMEM((4, 128, COLS), F32),
            pltpu.VMEM((2, 8, COLS), F32),
            pltpu.VMEM((2, 2, 2, 2, 8, 128), F32),
            pltpu.VMEM((2, 2, 2, RING - 1, 2, 8, 128), F32),
            pltpu.VMEM((2, 16, 128), F32),
            pltpu.VMEM((2, 4, 128, 128), F32),
            pltpu.VMEM((2, 8, 128), F32),
            pltpu.VMEM((2, 2 * XS - 1, 8, 128), F32),
            pltpu.VMEM((4, 128, 128), F32),
            pltpu.VMEM((4, 128, 128), F32),
            pltpu.VMEM((512, COLS), BF16),
            pltpu.VMEM((8, D, CH), F32),
            pltpu.VMEM((8, 7, 32, CH), F32),
            pltpu.VMEM((8, RING, 4, CH), F32),
            pltpu.VMEM((8, RING - 1, 4, CH), F32),
            pltpu.VMEM((2, 2, COLS), F32),
            pltpu.VMEM((2, COLS), F32),
            pltpu.VMEM((256, D), F32),
            pltpu.VMEM((256, D), F32),
            pltpu.VMEM((4, 64, D), F32),
            pltpu.VMEM((3, 64, D), F32),
            pltpu.VMEM((4, 64, D), F32),
            pltpu.SemaphoreType.DMA((2,)),
            pltpu.SemaphoreType.DMA((SEMS,)),
            pltpu.SemaphoreType.DMA((SEMS,)),
        ],
        compiler_params=pltpu.CompilerParams(
            collective_id=0, has_side_effects=True, vmem_limit_bytes=52 << 20
        ),
        cost_estimate=pl.CostEstimate(
            flops=2_000_000_000, bytes_accessed=4_000_000, transcendentals=1_100_000
        ),
    )(embeddings.reshape(4, 64, D), prototypes)
    return ge.reshape(2, 128, D), gp


def solution(mesh):
    return jax.shard_map(
        shards,
        mesh=mesh,
        in_specs=(P(None, "dp", None), P(None, "proto")),
        out_specs=(P(None, "dp", None), P("dp", "proto")),
        check_vma=False,
    )
```

time: 80.1 us -> 73.5 us (0.918)
  Pallas kernels: 75.4 us -> 70.4 us
  local copies, waits for them, and re-layouts: 3.81 us -> 2.22 us
    pallas_call x1, Pallas kernels: 75.4 us -> 70.4 us  [shards(): pl.pallas_call(kernel, name='swap_step', out_shape=(jax.ShapeDtypeStruct(...]
    unnamed x6 -> x4, local copies, waits for them, and re-layouts: 3.81 us -> 2.22 us
where the time goes in v2:
time: 73.5 us; the launch traced here: 73.3 us
  Pallas kernels  70.4 us (96%)
  local copies, waits for them, and re-layouts  2.22 us (3%)
    pallas_call x1, Pallas kernels, shards(): pl.pallas_call(kernel, name='swap_step', out_shape=(jax.ShapeDtypeStruct(...  70.4 us
    unnamed x4, local copies, waits for them, and re-layouts  2.22 us

profile of v2, /device:TPU:1, one launch (start us, length us, event | category | flops | bytes accessed | tf_op | source)
XLA Modules:
  0.0 73.3 jit_solution(13006806128358516212)
XLA Ops:
  0.6 0.0 copy-start
  0.6 0.9 %copy-done = bf16[2,128,256]{2,1,0:T(8,128)(2,1)S(1)} copy-done((bf16[2,128,256]{2,1,0:T(8,128)(2,1)S(1)}, bf16[2,128,256]{2,1,0:T(8,128)(2,1)}, u32[]{:S(2)}) %copy-start) | copy-done | bytes 131096
  1.5 70.4 %swap_step.1 = (f32[4,64,256]{2,1,0:T(8,128)S(1)}, f32[2,4096]{1,0:T(2,128)S(1)}) custom-call(bf16[4,64,256]{2,1,0:T(8,128)(2,1)S(1)} %bitcast.3, bf16[256,4096]{1,0:T(8,128)(2,1)} %proto_ref.1), custom_call_target="tpu_custom_call" | custom-call | flops 2000000000 | bytes 4000000 | tf_op jit(solution)/shard_map/swap_step/pallas_call | solution.py:475
  72.0 0.7 copy.6
  72.7 0.6 copy.7
Async XLA Ops:
  0.6 0.9 %copy-start = (bf16[2,128,256]{2,1,0:T(8,128)(2,1)S(1)}, bf16[2,128,256]{2,1,0:T(8,128)(2,1)}, u32[]{:S(2)}) copy-start(bf16[2,128,256]{2,1,0:T(8,128)(2,1)} %param.2) | copy-start | bytes 393220

commit v3 on v2

--- a/solution.py
+++ b/solution.py
@@ -15,6 +15,7 @@
 COLS = 2048
 HALF = 1024
 CH = 256
+CHUNKS = COLS // CH
 ORDER = (4, 3, 5, 2, 6, 1, 7)
 
 
@@ -382,25 +383,19 @@
             p2recv.at[ch],
         )
 
+    def terms(ch):
+        for q in range(4):
+            o = q + 1 - 2 * (q % 2)
+            for t in range(CH // 128):
+                cols = slice(chunks[ch][3] + t * 128, chunks[ch][3] + (t + 1) * 128)
+                g_ref[q * 128 : (q + 1) * 128, cols] = (
+                    e_ref[q, :, cols] - m_ref[o, :, cols] * rb[o]
+                ).astype(BF16)
+
+    terms(0)
     for ch, (_, _, h, col0, _) in enumerate(chunks):
-        def terms(i, carry):
-            slot = lax.div(i, 2)
-            for v in range(2):
-                q = slot * 2 + v
-                o = slot * 2 + 1 - v
-                for w in range(2):
-                    row0 = lax.rem(i, 2) * 64 + w * 32
-                    rows = pl.ds(pl.multiple_of(row0, 32), 32)
-                    r = rb[o, rows, :]
-                    to_rows = pl.ds(pl.multiple_of(q * 128 + row0, 32), 32)
-                    for t in range(CH // 128):
-                        cols = slice(col0 + t * 128, col0 + (t + 1) * 128)
-                        g_ref[to_rows, cols] = (
-                            e_ref[q, rows, cols] - m_ref[o, rows, cols] * r
-                        ).astype(BF16)
-            return carry
-
-        lax.fori_loop(0, 4, terms, 0)
+        if ch + 1 < len(chunks):
+            terms(ch + 1)
         gpart[ch] = jnp.dot(ut[h], g_ref[:, col0 : col0 + CH], preferred_element_type=F32)
         step0(ch)
 
@@ -501,10 +496,10 @@
             pltpu.VMEM((4, 128, 128), F32),
             pltpu.VMEM((4, 128, 128), F32),
             pltpu.VMEM((512, COLS), BF16),
-            pltpu.VMEM((8, D, CH), F32),
-            pltpu.VMEM((8, 7, 32, CH), F32),
-            pltpu.VMEM((8, RING, 4, CH), F32),
-            pltpu.VMEM((8, RING - 1, 4, CH), F32),
+            pltpu.VMEM((CHUNKS, D, CH), F32),
+            pltpu.VMEM((CHUNKS, 7, 32, CH), F32),
+            pltpu.VMEM((CHUNKS, RING, 4, CH), F32),
+            pltpu.VMEM((CHUNKS, RING - 1, 4, CH), F32),
             pltpu.VMEM((2, 2, COLS), F32),
             pltpu.VMEM((2, COLS), F32),
             pltpu.VMEM((256, D), F32),

time: 73.5 us -> 73.4 us (level)
  no operation moved by 1% of the time
where the time goes in v3:
time: 73.4 us; the launch traced here: 73.2 us
  Pallas kernels  70.4 us (96%)
  local copies, waits for them, and re-layouts  2.22 us (3%)
    pallas_call x1, Pallas kernels, shards(): pl.pallas_call(kernel, name='swap_step', out_shape=(jax.ShapeDtypeStruct(...  70.4 us
    unnamed x4, local copies, waits for them, and re-layouts  2.22 us

profile of v3, /device:TPU:1, one launch (start us, length us, event | category | flops | bytes accessed | tf_op | source)
XLA Modules:
  0.0 73.2 jit_solution(5122758598136829087)
XLA Ops:
  0.6 0.0 copy-start
  0.6 0.9 %copy-done = bf16[2,128,256]{2,1,0:T(8,128)(2,1)S(1)} copy-done((bf16[2,128,256]{2,1,0:T(8,128)(2,1)S(1)}, bf16[2,128,256]{2,1,0:T(8,128)(2,1)}, u32[]{:S(2)}) %copy-start) | copy-done | bytes 131096
  1.5 70.4 %swap_step.1 = (f32[4,64,256]{2,1,0:T(8,128)S(1)}, f32[2,4096]{1,0:T(2,128)S(1)}) custom-call(bf16[4,64,256]{2,1,0:T(8,128)(2,1)S(1)} %bitcast.3, bf16[256,4096]{1,0:T(8,128)(2,1)} %proto_ref.1), custom_call_target="tpu_custom_call" | custom-call | flops 2000000000 | bytes 4000000 | tf_op jit(solution)/shard_map/swap_step/pallas_call | solution.py:470
  71.9 0.7 copy.6
  72.6 0.6 copy.7
Async XLA Ops:
  0.6 0.9 %copy-start = (bf16[2,128,256]{2,1,0:T(8,128)(2,1)S(1)}, bf16[2,128,256]{2,1,0:T(8,128)(2,1)}, u32[]{:S(2)}) copy-start(bf16[2,128,256]{2,1,0:T(8,128)(2,1)} %param.2) | copy-start | bytes 393220

commit v4 on v3

--- a/solution.py
+++ b/solution.py
@@ -114,7 +114,7 @@
     )
     load.start()
 
-    row_peers = [(s // 2, s % 2) for s in range(1, 2 * XS)]
+    row_peers = [(2, 1), (2, 0), (1, 1), (3, 1), (1, 0), (3, 0), (0, 1)]
 
     def row_peer(dx, dc):
         return device(y, z, lax.rem(c + dc, 2), lax.rem(x + dx, XS))

time: 73.4 us -> 73.3 us (level)
  no operation moved by 1% of the time
where the time goes in v4:
time: 73.3 us; the launch traced here: 73.2 us
  Pallas kernels  70.3 us (96%)
  local copies, waits for them, and re-layouts  2.22 us (3%)
    pallas_call x1, Pallas kernels, shards(): pl.pallas_call(kernel, name='swap_step', out_shape=(jax.ShapeDtypeStruct(...  70.3 us
    unnamed x4, local copies, waits for them, and re-layouts  2.22 us

profile of v4, /device:TPU:1, one launch (start us, length us, event | category | flops | bytes accessed | tf_op | source)
XLA Modules:
  0.0 73.2 jit_solution(10088656475801876923)
XLA Ops:
  0.6 0.0 copy-start
  0.6 0.9 %copy-done = bf16[2,128,256]{2,1,0:T(8,128)(2,1)S(1)} copy-done((bf16[2,128,256]{2,1,0:T(8,128)(2,1)S(1)}, bf16[2,128,256]{2,1,0:T(8,128)(2,1)}, u32[]{:S(2)}) %copy-start) | copy-done | bytes 131096
  1.5 70.3 %swap_step.1 = (f32[4,64,256]{2,1,0:T(8,128)S(1)}, f32[2,4096]{1,0:T(2,128)S(1)}) custom-call(bf16[4,64,256]{2,1,0:T(8,128)(2,1)S(1)} %bitcast.3, bf16[256,4096]{1,0:T(8,128)(2,1)} %proto_ref.1), custom_call_target="tpu_custom_call" | custom-call | flops 2000000000 | bytes 4000000 | tf_op jit(solution)/shard_map/swap_step/pallas_call | solution.py:470
  71.8 0.7 copy.6
  72.5 0.6 copy.7
Async XLA Ops:
  0.6 0.9 %copy-start = (bf16[2,128,256]{2,1,0:T(8,128)(2,1)S(1)}, bf16[2,128,256]{2,1,0:T(8,128)(2,1)}, u32[]{:S(2)}) copy-start(bf16[2,128,256]{2,1,0:T(8,128)(2,1)} %param.2) | copy-start | bytes 393220
